TPU v7x, 256 devices: a whole 4x4x8 slice. The times are simulated.
256 devices in a mesh: slab: 64 (over z, y, core), tile: 4 (over x).
Axes of the slice: x: 4, y: 4, z: 8, core: 2. Of those that a mesh axis runs over, the one named last changes fastest.
Arguments:
- snapshots: bfloat16 [8192, 128, 256], P(('slab', 'tile')), may hold values from -1210 to 1210
- routes: int32 [8192, 1], P(('slab', 'tile')), may hold values from 0 to 3; in each aligned block of 32 rows (0 to 31, 32 to 63, ...) at most 10 rows name the same one
- sketch_matrix: bfloat16 [256, 128], replicated, may hold values from -0.375 to 0.375
Outputs:
- basis_rows: bfloat16 [10240, 128, 128], P(('slab', 'tile'))
- triangle: float32 [128, 128], replicated
Inputs may be any that keep to these rules, and one draw needn't show every extreme that they name: `routes`: among the 32 blocks of one device no owner value appears more than 10 times; a block with value o goes to tile o of its own slab.
All inputs are finite; a program needn't handle non-finite values.
Results may differ from a plain program's by a relative error of at most 0.0065.
Values may be sent and summed in bfloat16 or wider, within the bound.
A program may use at most 64 MiB of HBM per device.

v0:
```python
import math

import jax
import jax.numpy as jnp
from jax import lax
from jax.sharding import PartitionSpec as P

SEND = 10


def slot_selector(routes, tiles, slots):
    destination = routes[:, 0]
    owners = jnp.arange(tiles, dtype=jnp.int32)
    owner_hit = (destination[None, :] == owners[:, None]).astype(jnp.int32)
    earlier = jnp.cumsum(owner_hit, axis=1) - owner_hit
    slot_ids = jnp.arange(slots, dtype=jnp.int32)
    chosen = owner_hit[:, None, :] * (earlier[:, None, :] == slot_ids[None, :, None]).astype(
        jnp.int32
    )
    return chosen.reshape(tiles * slots, routes.shape[0]).astype(jnp.bfloat16)


def place_blocks(selector, block_data):
    block_count, cell_rows, width = block_data.shape
    flattened = jnp.dot(
        selector,
        block_data.reshape(block_count, cell_rows * width),
        preferred_element_type=jnp.float32,
    )
    return flattened.astype(jnp.bfloat16).reshape(selector.shape[0], cell_rows, width)


def global_factor(partial_gram):
    gram_matrix = lax.psum(partial_gram, ("slab", "tile"))
    return jnp.linalg.cholesky(gram_matrix)


def local(snapshots, routes, sketch_matrix):
    n_tile = lax.axis_size("tile")
    n_slab = lax.axis_size("slab")
    block_count, cell_rows, snap_width = snapshots.shape
    sketch_width = sketch_matrix.shape[1]
    cell_root = math.sqrt(block_count * cell_rows * n_slab * n_tile)
    selector = slot_selector(routes, n_tile, SEND)
    outgoing = place_blocks(selector, snapshots).reshape(n_tile, SEND, cell_rows, snap_width)
    product = jnp.einsum(
        "tjrc,cd->tjrd",
        lax.all_to_all(outgoing, "tile", split_axis=0, concat_axis=0, tiled=True),
        sketch_matrix,
        preferred_element_type=jnp.float32,
    )
    sketch = product.astype(jnp.bfloat16)
    sketch_rows = sketch.reshape(-1, sketch_width)
    partial_gram = lax.dot_general(
        sketch_rows, sketch_rows, (((0,), (0,)), ((), ())), preferred_element_type=jnp.float32
    )
    lower_factor = global_factor(partial_gram)
    identity = jnp.eye(sketch_width, dtype=jnp.float32)
    inverse_factor = jax.scipy.linalg.solve_triangular(lower_factor, identity, lower=True)
    wide_rows = sketch_rows.astype(jnp.float32)
    scaled = (
        jnp.dot(wide_rows, inverse_factor.T, precision=lax.Precision.HIGHEST) * cell_root
    ).astype(jnp.bfloat16)
    basis_rows = scaled.reshape(n_tile * SEND, cell_rows, sketch_width)
    return (basis_rows, lower_factor.T / cell_root)


def solution(mesh):
    return jax.shard_map(
        local,
        mesh=mesh,
        in_specs=(P(("slab", "tile"), None, None), P(("slab", "tile"), None), P()),
        out_specs=(P(("slab", "tile"), None, None), P()),
        check_vma=False,
    )
```

profile of v0, /device:TPU:1, one launch (start us, length us, event | category | flops | bytes accessed | tf_op | source)
XLA Modules:
  0.0 325.9 jit_solution(3418719268438397038)
XLA Ops:
  7.2 0.0 copy-start
  7.2 0.0 all-reduce.2.cloned.1.call-start
  7.2 0.7 fusion.5
  7.9 0.2 reduce_window_sum.11
  8.1 0.7 fusion.6
  8.8 2.8 copy.17
  11.6 0.8 convolution_convert_fusion
  12.4 0.6 copy.18
  13.0 35.5 %all_to_all.5 = bf16[4,10,128,256]{3,2,1,0:T(8,128)(2,1)S(1)} all-to-all(bf16[4,10,128,256]{3,2,1,0:T(8,128)(2,1)S(1)} %bitcast.35), channel_id=1, replica_groups=mesh['slab'=64,'tile'=4] {'tile'}, dimensions={0} | all-to-all | bytes 5242880 | tf_op jit(solution)/shard_map/all_to_all | solution.py:48
  48.6 0.0 copy-done
  48.6 0.8 convolution_convert_fusion.1
  49.4 1.2 convolution_bitcast_fusion
  50.6 0.0 all-reduce.2.cloned.1.call-update
  50.6 240.6 %all-reduce.2.cloned.1.call-done = f32[128,128]{0,1:T(8,128)} async-done(((f32[128,128]{0,1:T(8,128)}), f32[128,128]{0,1:T(8,128)}) %all-reduce.2.cloned.1.call-update) | async-done | bytes 65552 | tf_op jit(solution)/shard_map/psum | solution.py:34
  291.2 0.9 copy.11
  292.1 0.9 fusion.4
  293.0 11.7 %cholesky.17 = f32[128,128]{1,0:T(8,128)S(1)} custom-call(f32[128,128]{1,0:T(8,128)S(1)} %fusion.4), custom_call_target="Cholesky" | custom-call | tf_op jit(solution)/shard_map/jit(cholesky)/cholesky | solution.py:35
  304.7 0.6 compare_reduce_fusion
  305.4 0.7 multiply_bitcast_fusion
  306.0 0.7 copy.12
  306.8 9.8 %custom-call.7 = f32[1,128,128]{1,2,0:T(8,128)S(1)} custom-call(f32[1,128,128]{2,1,0:T(8,128)S(1)} %get-tuple-element.7), custom_call_target="InvertDiagBlocksLowerTriangular" | custom-call | tf_op jit(solution)/shard_map/jit(_solve_triangular)/triangular_solve | solution.py:59
  316.6 0.2 fusion.2
  316.8 2.3 fusion
  (3 shorter events, 0.1 us)
Async XLA Ops:
  7.2 41.4 %copy-start = (bf16[256,128]{1,0:T(8,128)(2,1)S(1)}, bf16[256,128]{1,0:T(8,128)(2,1)}, u32[]{:S(2)}) copy-start(bf16[256,128]{1,0:T(8,128)(2,1)} %param.5) | copy-start | bytes 196612
  7.2 284.0 %all-reduce.2.cloned.1.call-start = ((), (), s32[]{:S(2)}) async-start(), calls=%async_computation.1 | async-start | bytes 131072 | tf_op jit(solution)/shard_map/psum | solution.py:34
Sparse Core Ops, SparseCore 0:
  50.7 240.4 all-reduce.1
where the time goes:
time: 326 us
  waiting for transfers between devices  241 us (74%)
  blocking collectives  35.5 us (11%)
  other arithmetic  25.2 us (8%)
  between operations  14.1 us (4%)
  matrix products  5.37 us (2%)
  local copies, waits for them, and re-layouts  5.09 us (2%)
    psum x1, waiting for transfers between devices, global_factor(): gram_matrix = lax.psum(partial_gram, ('slab', 'tile'))  241 us
    all_to_all x1, blocking collectives, local(): lax.all_to_all(outgoing, 'tile', split_axis=0, concat_axis=0, tiled=True)  35.5 us
    another operation x3, other arithmetic, global_factor(): return jnp.linalg.cholesky(gram_matrix)  12.4 us
    another operation x1, other arithmetic, local(): jax.scipy.linalg.solve_triangular(lower_factor, identity, lower=True)  9.81 us
  transfers between devices with their start and end apart: 1, of which 1 were waited for; matrix products, arithmetic and copies ran while one was open for 0% of the time, Pallas kernels for 0%

commit v1 on v0

v1 whole, which is shorter than its diff:
```python
import functools
import math

import jax
import jax.numpy as jnp
from jax import lax
from jax.experimental import pallas as pl
from jax.experimental.pallas import tpu as pltpu
from jax.sharding import PartitionSpec as P

SEND = 10
TILES = 4
GROUP = 16
PIECES = 8
MESH = pl.DeviceIdType.MESH


def exchange(routes_ref, x_hbm, s_ref, placed_ref, gram_ref, x_ref, sk_ref, send_ref, part_ref, got1_ref, got2_ref,
             table_ref, x_sem, put_sem, get_sem, ar_put, ar_get):
    slab, tile = lax.axis_index("slab"), lax.axis_index("tile")
    core, y, z = slab % 2, (slab // 2) % 4, slab // 8
    ring = z * 2 + core
    face = y * 4 + tile

    def ring_peer(k):
        return (((k // 2) * 4 + y) * 2 + k % 2, tile)

    def face_peer(k):
        return ((z * 4 + k // 4) * 2 + core, k % 4)

    rows = x_hbm.shape[0] // PIECES

    def piece(p):
        part = pl.ds(p * rows, rows)
        return pltpu.make_async_copy(x_hbm.at[part], x_ref.at[part], x_sem.at[p])

    for p in range(PIECES):
        piece(p).start()

    barrier = pltpu.get_barrier_semaphore()

    @pl.loop(1, GROUP)
    def _(d):
        pl.semaphore_signal(barrier, inc=1, device_id=ring_peer((ring + d) % GROUP), device_id_type=MESH)
        pl.semaphore_signal(barrier, inc=1, device_id=face_peer((face + d) % GROUP), device_id_type=MESH)

    masks = [jnp.int32(0)] * TILES
    for j in range(32):
        route = routes_ref[0, j]
        bit = (1 << j) if j < 31 else -(1 << 31)
        masks = [jnp.where(route == o, m | jnp.int32(bit), m) for o, m in enumerate(masks)]
    for o in range(TILES):
        m = masks[o]
        for k in range(SEND):
            low = m & (-m)
            table_ref[o, k] = jnp.where(m != 0, 31 - lax.clz(low), -1)
            m = m & (m - 1)

    @pl.loop(0, PIECES)
    def _(p):
        piece(p).wait()
        wide = x_ref[pl.ds(p * rows, rows)].reshape(rows * 128, 256)
        sk = jnp.dot(wide, s_ref[...], preferred_element_type=jnp.float32)
        sk_ref[pl.ds(p * rows, rows)] = sk.astype(jnp.bfloat16).reshape(rows, 128, 128)

    pl.semaphore_wait(barrier, 2 * (GROUP - 1))

    def pick(o, k):
        at = table_ref[o, k]
        block = sk_ref[jnp.maximum(at, 0)]
        return jnp.where(at >= 0, block, jnp.zeros_like(block))

    def transfer(d):
        return pltpu.make_async_remote_copy(
            src_ref=send_ref.at[d - 1],
            dst_ref=placed_ref.at[tile],
            send_sem=put_sem.at[d - 1],
            recv_sem=get_sem.at[d - 1],
            device_id=(slab, (tile + d) % TILES),
            device_id_type=MESH,
        )

    for d in (2, 1, 3):
        @pl.loop(0, SEND)
        def _(k):
            send_ref[d - 1, k] = pick((tile + d) % TILES, k)
        transfer(d).start()

    part_ref[...] = jnp.zeros_like(part_ref)

    @pl.loop(0, PIECES)
    def _(p):
        sk = sk_ref[pl.ds(p * rows, rows)].reshape(rows * 128, 128)
        g = lax.dot_general(sk, sk, (((0,), (0,)), ((), ())), preferred_element_type=jnp.float32)
        part_ref[...] += g.reshape(GROUP, 8, 128)

    def all_of(ref, sem):
        return pltpu.make_async_copy(ref.at[pl.ds(0, GROUP - 1)], ref.at[pl.ds(0, GROUP - 1)], sem)

    def scatter(d):
        to = (ring + d) % GROUP
        return pltpu.make_async_remote_copy(
            src_ref=part_ref.at[to], dst_ref=got1_ref.at[d - 1], send_sem=ar_put.at[0], recv_sem=ar_get.at[0],
            device_id=ring_peer(to), device_id_type=MESH)

    @pl.loop(1, GROUP)
    def _(d):
        scatter(d).start()
    all_of(got1_ref, ar_get.at[0]).wait()
    mine = part_ref[ring]
    for d in range(GROUP - 1):
        mine = mine + got1_ref[d]
    got2_ref[face] = mine

    def swap(d):
        to = (face + d) % GROUP
        return pltpu.make_async_remote_copy(
            src_ref=got2_ref.at[face], dst_ref=got2_ref.at[face], send_sem=ar_put.at[1], recv_sem=ar_get.at[1],
            device_id=face_peer(to), device_id_type=MESH)

    @pl.loop(1, GROUP)
    def _(d):
        swap(d).start()
    all_of(got2_ref, ar_get.at[1]).wait()
    total = got2_ref[0]
    for d in range(1, GROUP):
        total = total + got2_ref[d]
    gram_ref[ring] = total

    def spread(d):
        to = (ring + d) % GROUP
        return pltpu.make_async_remote_copy(
            src_ref=gram_ref.at[ring], dst_ref=gram_ref.at[ring], send_sem=ar_put.at[2], recv_sem=ar_get.at[2],
            device_id=ring_peer(to), device_id_type=MESH)

    @pl.loop(1, GROUP)
    def _(d):
        spread(d).start()
    all_of(gram_ref, ar_get.at[2]).wait()

    @pl.loop(0, SEND)
    def _(k):
        placed_ref[tile, k] = pick(tile, k)
    for d in (1, 3, 2):
        transfer(d).wait()
    for i in range(3):
        all_of(got1_ref, ar_put.at[i]).wait()


def local(snapshots, routes, sketch_matrix):
    cell_root = math.sqrt(snapshots.shape[0] * 128 * lax.axis_size("slab") * lax.axis_size("tile"))
    vmem = pl.BlockSpec(memory_space=pltpu.VMEM)
    placed, gram = pl.pallas_call(
        exchange,
        out_shape=(
            jax.ShapeDtypeStruct((TILES, SEND, 128, 128), jnp.bfloat16),
            jax.ShapeDtypeStruct((GROUP, 8, 128), jnp.float32),
        ),
        in_specs=[pl.BlockSpec(memory_space=pltpu.SMEM), pl.BlockSpec(memory_space=pl.ANY), vmem],
        out_specs=(vmem, vmem),
        scratch_shapes=[
            pltpu.VMEM((32, 128, 256), jnp.bfloat16),
            pltpu.VMEM((32, 128, 128), jnp.bfloat16),
            pltpu.VMEM((TILES - 1, SEND, 128, 128), jnp.bfloat16),
            pltpu.VMEM((GROUP, 8, 128), jnp.float32),
            pltpu.VMEM((GROUP, 8, 128), jnp.float32),
            pltpu.VMEM((GROUP, 8, 128), jnp.float32),
            pltpu.SMEM((TILES, SEND), jnp.int32),
            pltpu.SemaphoreType.DMA((PIECES,)),
            pltpu.SemaphoreType.DMA((TILES - 1,)),
            pltpu.SemaphoreType.DMA((TILES - 1,)),
            pltpu.SemaphoreType.DMA((3,)),
            pltpu.SemaphoreType.DMA((3,)),
        ],
        compiler_params=pltpu.CompilerParams(collective_id=0, has_side_effects=True, vmem_limit_bytes=32 * 2**20),
        name="exchange",
    )(routes.reshape(1, 32), snapshots, sketch_matrix)
    lower = jnp.linalg.cholesky(gram.reshape(128, 128))
    inverse = jax.scipy.linalg.solve_triangular(lower, jnp.eye(128, dtype=jnp.float32), lower=True)
    rows = placed.reshape(-1, 128)
    basis = (jnp.dot(rows.astype(jnp.float32), inverse.T, precision=lax.Precision.HIGHEST) * cell_root).astype(jnp.bfloat16)
    return basis.reshape(TILES * SEND, 128, 128), lower.T / cell_root


def solution(mesh):
    return jax.shard_map(
        local,
        mesh=mesh,
        in_specs=(P(("slab", "tile"), None, None), P(("slab", "tile"), None), P()),
        out_specs=(P(("slab", "tile"), None, None), P()),
        check_vma=False,
    )
```

time: 326 us -> 65.3 us (0.20)
  waiting for transfers between devices: 241 us -> 0 us
  blocking collectives: 35.5 us -> 0 us
  Pallas kernels: 0 us -> 35.2 us
  between operations: 14.1 us -> 0.68 us
    psum x1 -> x0, waiting for transfers between devices: 241 us -> none  [global_factor(): gram_matrix = lax.psum(partial_gram, ('slab', 'tile'))]
    all_to_all x1 -> x0, blocking collectives: 35.5 us -> none  [local(): lax.all_to_all(outgoing, 'tile', split_axis=0, concat_axis=0, tiled=True)]
    pallas_call x0 -> x1, Pallas kernels: none -> 35.2 us  [local(): pl.pallas_call(exchange, out_shape=(jax.ShapeDtypeStruct((TILES, SEND, 12...]
    another operation x5 -> x4, other arithmetic: 22.4 us -> 22.2 us  [the longest x3 12.4 us: local(): lower = jnp.linalg.cholesky(gram.reshape(128, 128))]
  transfers between devices with their start and end apart: 1 -> 0, of which waited for: 1 -> 0; matrix products, arithmetic and copies ran while one was open for 0% -> 0% of each run, Pallas kernels for 0% -> 0%
where the time goes in v1:
time: 65.3 us; the launch traced here: 65.1 us
  Pallas kernels  35.2 us (54%)
  other arithmetic  22.9 us (35%)
  local copies, waits for them, and re-layouts  3.9 us (6%)
  matrix products  2.51 us (4%)
  between operations  0.68 us (1%)
    pallas_call x1, Pallas kernels, local(): pl.pallas_call(exchange, out_shape=(jax.ShapeDtypeStruct((TILES, SEND, 12...  35.2 us
    another operation x3, other arithmetic, local(): lower = jnp.linalg.cholesky(gram.reshape(128, 128))  12.4 us
    another operation x1, other arithmetic, local(): jax.scipy.linalg.solve_triangular(lower, jnp.eye(128, dtype=jnp.float32),...  9.81 us
    unnamed x7, local copies, waits for them, and re-layouts  3.81 us
    dot_general x1, matrix products, local(): jnp.dot(rows.astype(jnp.float32), inverse.T, precision=lax.Precision.HIGH...  2.26 us

profile of v1, /device:TPU:1, one launch (start us, length us, event | category | flops | bytes accessed | tf_op | source)
XLA Modules:
  0.0 65.1 jit_solution(10253507372189793915)
XLA Ops:
  0.6 0.0 copy-start
  0.6 1.6 %copy-done = bf16[32,128,256]{2,1,0:T(8,128)(2,1)S(1)} copy-done((bf16[32,128,256]{2,1,0:T(8,128)(2,1)S(1)}, bf16[32,128,256]{2,1,0:T(8,128)(2,1)}, u32[]{:S(2)}) %copy-start) | copy-done | bytes 2097176
  2.2 0.0 copy-start.1
  2.2 0.8 %copy-done.1 = bf16[256,128]{1,0:T(8,128)(2,1)S(1)} copy-done((bf16[256,128]{1,0:T(8,128)(2,1)S(1)}, bf16[256,128]{1,0:T(8,128)(2,1)}, u32[]{:S(2)}) %copy-start.1) | copy-done | bytes 65560
  3.1 0.0 copy-start.2
  3.1 0.7 %copy-done.2 = s32[32,1]{0,1:T(1,128)S(1)} copy-done((s32[32,1]{0,1:T(1,128)S(1)}, s32[32,1]{0,1:T(1,128)}, u32[]{:S(2)}) %copy-start.2) | copy-done | bytes 152
  3.7 35.2 %exchange.1 = (bf16[4,10,128,128]{3,2,1,0:T(8,128)(2,1)S(1)}, f32[16,8,128]{2,1,0:T(8,128)S(1)}) custom-call(s32[1,32]{1,0:T(1,128)S(1)} %bitcast.20, bf16[32,128,256]{2,1,0:T(8,128)(2,1)S(1)} %copy-done, bf16[256,128]{1,0:T(8,128)(2,1)S(1)} %copy-done.1), custom_call_target="tpu_custom_call" | custom-call | tf_op jit(solution)/shard_map/exchange/pallas_call | solution.py:153
  38.9 0.1 copy.8
  39.0 11.7 %cholesky.17 = f32[128,128]{1,0:T(8,128)S(1)} custom-call(f32[128,128]{1,0:T(8,128)S(1)} %fusion.3), custom_call_target="Cholesky" | custom-call | tf_op jit(solution)/shard_map/jit(cholesky)/cholesky | solution.py:178
  50.8 0.6 compare_reduce_fusion
  51.4 0.7 %multiply_bitcast_fusion = (f32[128,128]{0,1:T(8,128)S(1)}, f32[1,128,128]{2,1,0:T(8,128)S(1)}) fusion(f32[128,128]{1,0:T(8,128)S(1)} %cholesky.17, pred[]{:T(512)} %compare_reduce_fusion), kind=kLoop, calls=%fused_computation.6 | loop fusion | flops 81920 | bytes 196609 | tf_op jit(solution)/shard_map/div | solution.py:182
  52.1 0.7 %copy.9 = f32[128,128]{1,0:T(8,128)} copy(f32[128,128]{0,1:T(8,128)S(1)} %get-tuple-element.10) | data formatting | bytes 131072
  52.8 9.8 %custom-call.7 = f32[1,128,128]{1,2,0:T(8,128)S(1)} custom-call(f32[1,128,128]{2,1,0:T(8,128)S(1)} %get-tuple-element.11), custom_call_target="InvertDiagBlocksLowerTriangular" | custom-call | tf_op jit(solution)/shard_map/jit(_solve_triangular)/triangular_solve | solution.py:179
  62.6 0.2 fusion.1
  62.9 2.3 %fusion = bf16[5120,128]{1,0:T(8,128)(2,1)} fusion(bf16[5120,128]{1,0:T(8,128)(2,1)S(1)} %bitcast.18, f32[128,128]{1,0:T(8,128)S(1)} %fusion.1), kind=kOutput, calls=%fused_computation.1 | convolution fusion | flops 1007943680 | bytes 2686976 | tf_op jit(solution)/shard_map/dot_general | solution.py:181
  (2 shorter events, 0.0 us)
Async XLA Ops:
  0.6 1.6 %copy-start = (bf16[32,128,256]{2,1,0:T(8,128)(2,1)S(1)}, bf16[32,128,256]{2,1,0:T(8,128)(2,1)}, u32[]{:S(2)}) copy-start(bf16[32,128,256]{2,1,0:T(8,128)(2,1)} %x_hbm.1) | copy-start | bytes 6291460
  2.2 0.8 %copy-start.1 = (bf16[256,128]{1,0:T(8,128)(2,1)S(1)}, bf16[256,128]{1,0:T(8,128)(2,1)}, u32[]{:S(2)}) copy-start(bf16[256,128]{1,0:T(8,128)(2,1)} %s_ref.1) | copy-start | bytes 196612
  3.1 0.7 %copy-start.2 = (s32[32,1]{0,1:T(1,128)S(1)}, s32[32,1]{0,1:T(1,128)}, u32[]{:S(2)}) copy-start(s32[32,1]{0,1:T(1,128)} %param.4) | copy-start | bytes 388

commit v2 on v1

v2 whole, which is shorter than its diff:
```python
import math

import jax
import jax.numpy as jnp
from jax import lax
from jax.experimental import pallas as pl
from jax.experimental.pallas import tpu as pltpu
from jax.sharding import PartitionSpec as P

SEND = 10
TILES = 4
GROUP = 16
PIECES = 8
STEPS = 8
FIRST = ((1, 0), (3, 0))
LATER = ((2, 0), (2, 1), (1, 1), (3, 1))
MESH = pl.DeviceIdType.MESH
F32, BF16 = jnp.float32, jnp.bfloat16


def split3(v):
    h = v.astype(BF16)
    rest = v - h.astype(F32)
    m = rest.astype(BF16)
    return h, m, (rest - m.astype(F32)).astype(BF16)


def outer_products(u):
    h, m, l = split3(u)
    left = jnp.concatenate([v[:, :128] for v in (h, h, m, h, l, m)], 0)
    right = jnp.concatenate([h, m, h, l, h, m], 0)
    return lax.dot_general(left, right, (((0,), (0,)), ((), ())), preferred_element_type=F32)


def factor(gram_ref, upper_ref, inverse_ref, work):
    row = lax.broadcasted_iota(jnp.int32, (128, 128), 0)
    col = lax.broadcasted_iota(jnp.int32, (128, 128), 1)
    work[:, :128] = gram_ref[...].reshape(128, 128)
    work[:, 128:] = (row == col).astype(F32)
    sub = lax.broadcasted_iota(jnp.int32, (8, 256), 0)
    for p in range(GROUP):
        panel = work[8 * p : 8 * p + 8, :]
        e = {}
        for k in range(8):
            c = jnp.broadcast_to(panel[:, 8 * p + k : 8 * p + k + 1], (8, 128))
            for i in range(k, 8):
                e[i, k] = jnp.broadcast_to(c[i : i + 1], (8, 128))
        x = [jnp.broadcast_to(panel[i : i + 1], (8, 256)) for i in range(8)]
        for k in range(8):
            r = lax.rsqrt(e[k, k])
            l = {i: e[i, k] * r for i in range(k + 1, 8)}
            x[k] = x[k] * jnp.concatenate([r, r], 1)
            for i in range(k + 1, 8):
                for j in range(k + 1, i + 1):
                    e[i, j] = e[i, j] - l[i] * l[j]
                x[i] = x[i] - jnp.concatenate([l[i], l[i]], 1) * x[k]
        u = x[0]
        for k in range(1, 8):
            u = jnp.where(sub == k, x[k], u)
        upper_ref[8 * p : 8 * p + 8, :] = u[:, :128]
        inverse_ref[8 * p : 8 * p + 8, :] = u[:, 128:]
        if p < GROUP - 1:
            g = outer_products(u)
            work[8 * p + 8 :, :] = work[8 * p + 8 :, :] - g[8 * p + 8 :, :]


def exchange(routes_hbm, x_hbm, s_hbm, placed_ref, upper_ref, inverse_ref, x_ref, s_ref, routes_ref, sk_ref, send_ref, part_ref,
             got1_ref, got2_ref, gram_ref, work_ref, table_ref, x_sem, in_sem, put_sem, get_sem, ar_put, ar_get):
    slab, tile = lax.axis_index("slab"), lax.axis_index("tile")
    core, y, z = slab % 2, (slab // 2) % 4, slab // 8
    ring = z * 2 + core
    face = y * 4 + tile

    def ring_peer(k):
        return (((k // 2) * 4 + y) * 2 + k % 2, tile)

    def face_peer(k):
        return ((z * 4 + k // 4) * 2 + core, k % 4)

    rows = x_hbm.shape[0] // PIECES

    def piece(p):
        part = pl.ds(p * rows, rows)
        return pltpu.make_async_copy(x_hbm.at[part], x_ref.at[part], x_sem.at[p])

    s_copy = pltpu.make_async_copy(s_hbm, s_ref, in_sem.at[0])
    routes_copy = pltpu.make_async_copy(routes_hbm, routes_ref, in_sem.at[1])
    s_copy.start()
    for p in range(PIECES):
        piece(p).start()
    routes_copy.start()

    barrier = pltpu.get_barrier_semaphore()
    for d in range(1, GROUP):
        pl.semaphore_signal(barrier, inc=1, device_id=ring_peer((ring + d) % GROUP), device_id_type=MESH)
        pl.semaphore_signal(barrier, inc=1, device_id=face_peer((face + d) % GROUP), device_id_type=MESH)

    part_ref[...] = jnp.zeros_like(part_ref)
    s_copy.wait()

    @pl.loop(0, PIECES)
    def _(p):
        piece(p).wait()
        wide = x_ref[pl.ds(p * rows, rows)].reshape(rows * 128, 256)
        sk = jnp.dot(wide, s_ref[...], preferred_element_type=F32).astype(BF16)
        sk_ref[pl.ds(p * rows, rows)] = sk.reshape(rows, 128, 128)
        g = lax.dot_general(sk, sk, (((0,), (0,)), ((), ())), preferred_element_type=F32)
        part_ref[...] += g.reshape(GROUP, 8, 128)

    pl.semaphore_wait(barrier, 2 * (GROUP - 1))

    def all_of(ref, sem):
        return pltpu.make_async_copy(ref.at[pl.ds(0, GROUP - 1)], ref.at[pl.ds(0, GROUP - 1)], sem)

    for d in range(1, GROUP):
        to = (ring + d) % GROUP
        pltpu.make_async_remote_copy(
            src_ref=part_ref.at[to], dst_ref=got1_ref.at[d - 1], send_sem=ar_put.at[0], recv_sem=ar_get.at[0],
            device_id=ring_peer(to), device_id_type=MESH).start()

    routes_copy.wait()
    masks = [jnp.int32(0)] * TILES
    for j in range(32):
        route = routes_ref[0, j]
        bit = (1 << j) if j < 31 else -(1 << 31)
        masks = [jnp.where(route == o, m | jnp.int32(bit), m) for o, m in enumerate(masks)]
    for o in range(TILES):
        m = masks[o]
        for k in range(SEND):
            low = m & (-m)
            table_ref[o, k] = jnp.where(m != 0, 31 - lax.clz(low), -1)
            m = m & (m - 1)

    def pick(o, k):
        at = table_ref[o, k]
        block = sk_ref[jnp.maximum(at, 0)]
        return jnp.where(at >= 0, block, jnp.zeros_like(block))

    half = SEND // 2

    def transfer(d, h):
        return pltpu.make_async_remote_copy(
            src_ref=send_ref.at[d - 1, pl.ds(h * half, half)],
            dst_ref=placed_ref.at[tile, pl.ds(h * half, half)],
            send_sem=put_sem.at[d - 1, h],
            recv_sem=get_sem.at[d - 1, h],
            device_id=(slab, (tile + d) % TILES),
            device_id_type=MESH,
        )

    def fill(d, h):
        @pl.loop(h * half, (h + 1) * half)
        def _(k):
            send_ref[d - 1, k] = pick((tile + d) % TILES, k)

    for d, h in FIRST:
        fill(d, h)
        transfer(d, h).start()
    for d, h in LATER:
        fill(d, h)

    @pl.loop(0, SEND)
    def _(k):
        placed_ref[tile, k] = pick(tile, k)

    all_of(got1_ref, ar_get.at[0]).wait()
    mine = part_ref[ring]
    for d in range(GROUP - 1):
        mine = mine + got1_ref[d]
    got2_ref[face] = mine
    for d in range(1, GROUP):
        to = (face + d) % GROUP
        pltpu.make_async_remote_copy(
            src_ref=got2_ref.at[face], dst_ref=got2_ref.at[face], send_sem=ar_put.at[1], recv_sem=ar_get.at[1],
            device_id=face_peer(to), device_id_type=MESH).start()
    all_of(got2_ref, ar_get.at[1]).wait()
    total = got2_ref[0]
    for d in range(1, GROUP):
        total = total + got2_ref[d]
    gram_ref[ring] = total
    for d in range(1, GROUP):
        to = (ring + d) % GROUP
        pltpu.make_async_remote_copy(
            src_ref=gram_ref.at[ring], dst_ref=gram_ref.at[ring], send_sem=ar_put.at[2], recv_sem=ar_get.at[2],
            device_id=ring_peer(to), device_id_type=MESH).start()
    for d, h in LATER:
        transfer(d, h).start()
    all_of(gram_ref, ar_get.at[2]).wait()

    factor(gram_ref, upper_ref, inverse_ref, work_ref)

    for i in range(3):
        all_of(got1_ref, ar_put.at[i]).wait()
    for d, h in FIRST + LATER:
        transfer(d, h).wait()


def scale(cell_root, placed_ref, upper_ref, inverse_ref, basis_hbm, triangle_hbm, basis_ref, triangle_ref, sem, tri_sem):
    row = lax.broadcasted_iota(jnp.int32, (128, 128), 0)
    col = lax.broadcasted_iota(jnp.int32, (128, 128), 1)
    triangle_ref[...] = jnp.where(row <= col, upper_ref[...] * (1.0 / cell_root), 0.0)
    tri = pltpu.make_async_copy(triangle_ref, triangle_hbm, tri_sem)
    tri.start()
    h, m, l = split3(jnp.where(row >= col, inverse_ref[...] * cell_root, 0.0))
    count = placed_ref.shape[0] // STEPS

    def copy(i):
        part = pl.ds(i * count, count)
        return pltpu.make_async_copy(basis_ref.at[part], basis_hbm.at[part], sem.at[i])

    for i in range(STEPS):
        part = pl.ds(i * count, count)
        rows = placed_ref[part].reshape(count * 128, 128)
        out = sum(lax.dot_general(rows, w, (((1,), (1,)), ((), ())), preferred_element_type=F32) for w in (l, m, h))
        basis_ref[part] = out.astype(BF16).reshape(count, 128, 128)
        copy(i).start()
    tri.wait()
    for i in range(STEPS):
        copy(i).wait()


def local(snapshots, routes, sketch_matrix):
    cell_root = math.sqrt(snapshots.shape[0] * 128 * lax.axis_size("slab") * lax.axis_size("tile"))
    vmem = pl.BlockSpec(memory_space=pltpu.VMEM)
    hbm = pl.BlockSpec(memory_space=pltpu.HBM)
    square = jax.ShapeDtypeStruct((128, 128), F32)
    placed, upper, inverse = pl.pallas_call(
        exchange,
        out_shape=(jax.ShapeDtypeStruct((TILES, SEND, 128, 128), BF16), square, square),
        in_specs=[hbm, hbm, hbm],
        out_specs=(vmem, vmem, vmem),
        scratch_shapes=[
            pltpu.VMEM((32, 128, 256), BF16),
            pltpu.VMEM((256, 128), BF16),
            pltpu.SMEM((1, 32), jnp.int32),
            pltpu.VMEM((32, 128, 128), BF16),
            pltpu.VMEM((TILES - 1, SEND, 128, 128), BF16),
            pltpu.VMEM((GROUP, 8, 128), F32),
            pltpu.VMEM((GROUP, 8, 128), F32),
            pltpu.VMEM((GROUP, 8, 128), F32),
            pltpu.VMEM((GROUP, 8, 128), F32),
            pltpu.VMEM((128, 256), F32),
            pltpu.SMEM((TILES, SEND), jnp.int32),
            pltpu.SemaphoreType.DMA((PIECES,)),
            pltpu.SemaphoreType.DMA((2,)),
            pltpu.SemaphoreType.DMA((TILES - 1, 2)),
            pltpu.SemaphoreType.DMA((TILES - 1, 2)),
            pltpu.SemaphoreType.DMA((3,)),
            pltpu.SemaphoreType.DMA((3,)),
        ],
        compiler_params=pltpu.CompilerParams(collective_id=0, has_side_effects=True, vmem_limit_bytes=32 * 2**20),
        name="exchange",
    )(*(pltpu.with_memory_space_constraint(v, pltpu.HBM) for v in (routes.reshape(1, 32), snapshots, sketch_matrix)))
    return tuple(pl.pallas_call(
        lambda *refs: scale(cell_root, *refs),
        out_shape=(jax.ShapeDtypeStruct((TILES * SEND, 128, 128), BF16), square),
        in_specs=[vmem, vmem, vmem],
        out_specs=(hbm, hbm),
        scratch_shapes=[
            pltpu.VMEM((TILES * SEND, 128, 128), BF16),
            pltpu.VMEM((128, 128), F32),
            pltpu.SemaphoreType.DMA((STEPS,)),
            pltpu.SemaphoreType.DMA,
        ],
        compiler_params=pltpu.CompilerParams(vmem_limit_bytes=32 * 2**20),
        name="scale",
    )(placed.reshape(TILES * SEND, 128, 128), upper, inverse))


def solution(mesh):
    return jax.shard_map(
        local,
        mesh=mesh,
        in_specs=(P(("slab", "tile"), None, None), P(("slab", "tile"), None), P()),
        out_specs=(P(("slab", "tile"), None, None), P()),
        check_vma=False,
    )
```

time: 65.3 us -> 37.3 us (0.57)
  other arithmetic: 22.9 us -> 0 us
  local copies, waits for them, and re-layouts: 3.9 us -> 0 us
  matrix products: 2.51 us -> 0 us
  Pallas kernels: 35.2 us -> 36.6 us
    another operation x4 -> x0, other arithmetic: 22.2 us -> none  [the longest x3 12.4 us: local(): lower = jnp.linalg.cholesky(gram.reshape(128, 128))]
    unnamed x7 -> x0, local copies, waits for them, and re-layouts: 3.81 us -> none
    dot_general x1 -> x0, matrix products: 2.26 us -> none  [local(): jnp.dot(rows.astype(jnp.float32), inverse.T, precision=lax.Precision.HIGH...]
    pallas_call x0 -> x1, Pallas kernels: none -> 2 us  [local(): pl.pallas_call(lambda *refs: scale(cell_root, *refs), out_shape=(jax.Shap...]
    div x2 -> x0, other arithmetic: 0.67 us -> none  [the longest x1 0.66 us: local(): return (basis.reshape(TILES * SEND, 128, 128), lower.T / cell_root)]
where the time goes in v2:
time: 37.3 us; the launch traced here: 37.2 us
  Pallas kernels  36.6 us (98%)
  between operations  0.64 us (2%)
    pallas_call x1, Pallas kernels, local(): pl.pallas_call(exchange, out_shape=(jax.ShapeDtypeStruct((TILES, SEND, 12...  34.6 us
    pallas_call x1, Pallas kernels, local(): pl.pallas_call(lambda *refs: scale(cell_root, *refs), out_shape=(jax.Shap...  2 us

profile of v2, /device:TPU:1, one launch (start us, length us, event | category | flops | bytes accessed | tf_op | source)
XLA Modules:
  0.0 37.2 jit_solution(12282937427379767640)
XLA Ops:
  0.6 34.6 %exchange.1 = (bf16[4,10,128,128]{3,2,1,0:T(8,128)(2,1)S(1)}, f32[128,128]{1,0:T(8,128)S(1)}, f32[128,128]{1,0:T(8,128)S(1)}) custom-call(s32[1,32]{1,0:T(1,128)} %bitcast.3, bf16[32,128,256]{2,1,0:T(8,128)(2,1)} %x_hbm.1, bf16[256,128]{1,0:T(8,128)(2,1)} %s_hbm.1), custom_call_target="tpu_custom_call" | custom-call | tf_op jit(solution)/shard_map/exchange/pallas_call | solution.py:227
  35.2 2.0 %scale.1 = (bf16[40,128,128]{2,1,0:T(8,128)(2,1)}, f32[128,128]{1,0:T(8,128)}) custom-call(bf16[40,128,128]{2,1,0:T(8,128)(2,1)S(1)} %bitcast.2, f32[128,128]{1,0:T(8,128)S(1)} %get-tuple-element.6.refs_1_, f32[128,128]{1,0:T(8,128)S(1)} %get-tuple-element.7.refs_2_), custom_call_target="tpu_custom_call" | custom-call | tf_op jit(solution)/shard_map/scale/pallas_call | solution.py:254

commit v3 on v2

--- a/solution.py
+++ b/solution.py
@@ -12,8 +12,8 @@
 GROUP = 16
 PIECES = 8
 STEPS = 8
-FIRST = ((1, 0), (3, 0))
-LATER = ((2, 0), (2, 1), (1, 1), (3, 1))
+SPAN = 64
+START = (((2, 0, 5),), ((2, 5, 5), (1, 0, 10), (3, 0, 10)), ())
 MESH = pl.DeviceIdType.MESH
 F32, BF16 = jnp.float32, jnp.bfloat16
 
@@ -30,6 +30,18 @@
     left = jnp.concatenate([v[:, :128] for v in (h, h, m, h, l, m)], 0)
     right = jnp.concatenate([h, m, h, l, h, m], 0)
     return lax.dot_general(left, right, (((0,), (0,)), ((), ())), preferred_element_type=F32)
+
+
+def line(v, i):
+    return jnp.broadcast_to(v[i : i + 1], (8, v.shape[1]))
+
+
+def columns(rows, p):
+    return [jnp.broadcast_to(rows[:, p + k : p + k + 1], (8, 128)) for k in range(8)]
+
+
+def wide(v):
+    return jnp.concatenate([v, v], 1)
 
 
 def factor(gram_ref, upper_ref, inverse_ref, work):
@@ -38,30 +50,41 @@
     work[:, :128] = gram_ref[...].reshape(128, 128)
     work[:, 128:] = (row == col).astype(F32)
     sub = lax.broadcasted_iota(jnp.int32, (8, 256), 0)
-    for p in range(GROUP):
-        panel = work[8 * p : 8 * p + 8, :]
-        e = {}
-        for k in range(8):
-            c = jnp.broadcast_to(panel[:, 8 * p + k : 8 * p + k + 1], (8, 128))
-            for i in range(k, 8):
-                e[i, k] = jnp.broadcast_to(c[i : i + 1], (8, 128))
-        x = [jnp.broadcast_to(panel[i : i + 1], (8, 256)) for i in range(8)]
-        for k in range(8):
-            r = lax.rsqrt(e[k, k])
-            l = {i: e[i, k] * r for i in range(k + 1, 8)}
-            x[k] = x[k] * jnp.concatenate([r, r], 1)
-            for i in range(k + 1, 8):
-                for j in range(k + 1, i + 1):
-                    e[i, j] = e[i, j] - l[i] * l[j]
-                x[i] = x[i] - jnp.concatenate([l[i], l[i]], 1) * x[k]
-        u = x[0]
-        for k in range(1, 8):
-            u = jnp.where(sub == k, x[k], u)
-        upper_ref[8 * p : 8 * p + 8, :] = u[:, :128]
-        inverse_ref[8 * p : 8 * p + 8, :] = u[:, 128:]
-        if p < GROUP - 1:
-            g = outer_products(u)
-            work[8 * p + 8 :, :] = work[8 * p + 8 :, :] - g[8 * p + 8 :, :]
+    for s in range(0, 128, SPAN):
+        rows = {q: work[q : q + 8, :] for q in range(s, s + SPAN, 8)}
+        own = columns(rows[s], s)
+        done = []
+        for p in range(s, s + SPAN, 8):
+            later = range(p + 8, s + SPAN, 8)
+            cols = {q: columns(rows[q], p) for q in later}
+            e = {(i, k): line(own[k], i) for k in range(8) for i in range(k, 8)}
+            own = columns(rows[p + 8], p + 8) if later else None
+            x = [line(rows[p], i) for i in range(8)]
+            for k in range(8):
+                r = lax.rsqrt(e[k, k])
+                l = {i: e[i, k] * r for i in range(k + 1, 8)}
+                for i in range(k + 1, 8):
+                    for j in range(k + 1, i + 1):
+                        e[i, j] = e[i, j] - l[i] * l[j]
+                x[k] = x[k] * wide(r)
+                for i in range(k + 1, 8):
+                    x[i] = x[i] - wide(l[i]) * x[k]
+                for q in later:
+                    m = cols[q][k] * r
+                    if q == p + 8:
+                        own = [o - m * line(m, j) for j, o in enumerate(own)]
+                    for j in range(k + 1, 8):
+                        cols[q][j] = cols[q][j] - m * l[j]
+                    rows[q] = rows[q] - wide(m) * x[k]
+            u = x[0]
+            for k in range(1, 8):
+                u = jnp.where(sub == k, x[k], u)
+            upper_ref[p : p + 8, :] = u[:, :128]
+            inverse_ref[p : p + 8, :] = u[:, 128:]
+            done.append(u)
+        if s + SPAN < 128:
+            g = outer_products(jnp.concatenate(done, 0))
+            work[s + SPAN :, :] = work[s + SPAN :, :] - g[s + SPAN :, :]
 
 
 def exchange(routes_hbm, x_hbm, s_hbm, placed_ref, upper_ref, inverse_ref, x_ref, s_ref, routes_ref, sk_ref, send_ref, part_ref,
@@ -136,28 +159,29 @@
         block = sk_ref[jnp.maximum(at, 0)]
         return jnp.where(at >= 0, block, jnp.zeros_like(block))
 
-    half = SEND // 2
-
-    def transfer(d, h):
+    parts = [part for step in START for part in step]
+
+    def transfer(d, first, count):
+        at = parts.index((d, first, count))
         return pltpu.make_async_remote_copy(
-            src_ref=send_ref.at[d - 1, pl.ds(h * half, half)],
-            dst_ref=placed_ref.at[tile, pl.ds(h * half, half)],
-            send_sem=put_sem.at[d - 1, h],
-            recv_sem=get_sem.at[d - 1, h],
+            src_ref=send_ref.at[d - 1, pl.ds(first, count)],
+            dst_ref=placed_ref.at[tile, pl.ds(first, count)],
+            send_sem=put_sem.at[at],
+            recv_sem=get_sem.at[at],
             device_id=(slab, (tile + d) % TILES),
             device_id_type=MESH,
         )
 
-    def fill(d, h):
-        @pl.loop(h * half, (h + 1) * half)
+    def fill(d, first, count):
+        @pl.loop(first, first + count)
         def _(k):
             send_ref[d - 1, k] = pick((tile + d) % TILES, k)
 
-    for d, h in FIRST:
-        fill(d, h)
-        transfer(d, h).start()
-    for d, h in LATER:
-        fill(d, h)
+    for part in START[0]:
+        fill(*part)
+        transfer(*part).start()
+    for part in parts[len(START[0]):]:
+        fill(*part)
 
     @pl.loop(0, SEND)
     def _(k):
@@ -173,6 +197,8 @@
         pltpu.make_async_remote_copy(
             src_ref=got2_ref.at[face], dst_ref=got2_ref.at[face], send_sem=ar_put.at[1], recv_sem=ar_get.at[1],
             device_id=face_peer(to), device_id_type=MESH).start()
+    for part in START[1]:
+        transfer(*part).start()
     all_of(got2_ref, ar_get.at[1]).wait()
     total = got2_ref[0]
     for d in range(1, GROUP):
@@ -183,16 +209,16 @@
         pltpu.make_async_remote_copy(
             src_ref=gram_ref.at[ring], dst_ref=gram_ref.at[ring], send_sem=ar_put.at[2], recv_sem=ar_get.at[2],
             device_id=ring_peer(to), device_id_type=MESH).start()
-    for d, h in LATER:
-        transfer(d, h).start()
+    for part in START[2]:
+        transfer(*part).start()
     all_of(gram_ref, ar_get.at[2]).wait()
 
     factor(gram_ref, upper_ref, inverse_ref, work_ref)
 
     for i in range(3):
         all_of(got1_ref, ar_put.at[i]).wait()
-    for d, h in FIRST + LATER:
-        transfer(d, h).wait()
+    for part in parts:
+        transfer(*part).wait()
 
 
 def scale(cell_root, placed_ref, upper_ref, inverse_ref, basis_hbm, triangle_hbm, basis_ref, triangle_ref, sem, tri_sem):
@@ -243,8 +269,8 @@
             pltpu.SMEM((TILES, SEND), jnp.int32),
             pltpu.SemaphoreType.DMA((PIECES,)),
             pltpu.SemaphoreType.DMA((2,)),
-            pltpu.SemaphoreType.DMA((TILES - 1, 2)),
-            pltpu.SemaphoreType.DMA((TILES - 1, 2)),
+            pltpu.SemaphoreType.DMA((sum(map(len, START)),)),
+            pltpu.SemaphoreType.DMA((sum(map(len, START)),)),
             pltpu.SemaphoreType.DMA((3,)),
             pltpu.SemaphoreType.DMA((3,)),
         ],

time: 37.3 us -> 33.3 us (0.89)
  Pallas kernels: 36.6 us -> 32.5 us
    pallas_call x1, Pallas kernels: 34.6 us -> 30.5 us  [local(): pl.pallas_call(exchange, out_shape=(jax.ShapeDtypeStruct((TILES, SEND, 12...]
where the time goes in v3:
time: 33.3 us; the launch traced here: 33.2 us
  Pallas kernels  32.5 us (98%)
  between operations  0.64 us (2%)
    pallas_call x1, Pallas kernels, local(): pl.pallas_call(exchange, out_shape=(jax.ShapeDtypeStruct((TILES, SEND, 12...  30.5 us
    pallas_call x1, Pallas kernels, local(): pl.pallas_call(lambda *refs: scale(cell_root, *refs), out_shape=(jax.Shap...  2 us

profile of v3, /device:TPU:1, one launch (start us, length us, event | category | flops | bytes accessed | tf_op | source)
XLA Modules:
  0.0 33.2 jit_solution(15223018414255310241)
XLA Ops:
  0.6 30.5 %exchange.1 = (bf16[4,10,128,128]{3,2,1,0:T(8,128)(2,1)S(1)}, f32[128,128]{1,0:T(8,128)S(1)}, f32[128,128]{1,0:T(8,128)S(1)}) custom-call(s32[1,32]{1,0:T(1,128)} %bitcast.3, bf16[32,128,256]{2,1,0:T(8,128)(2,1)} %x_hbm.1, bf16[256,128]{1,0:T(8,128)(2,1)} %s_hbm.1), custom_call_target="tpu_custom_call" | custom-call | tf_op jit(solution)/shard_map/exchange/pallas_call | solution.py:253
  31.2 2.0 %scale.1 = (bf16[40,128,128]{2,1,0:T(8,128)(2,1)}, f32[128,128]{1,0:T(8,128)}) custom-call(bf16[40,128,128]{2,1,0:T(8,128)(2,1)S(1)} %bitcast.2, f32[128,128]{1,0:T(8,128)S(1)} %get-tuple-element.6.refs_1_, f32[128,128]{1,0:T(8,128)S(1)} %get-tuple-element.7.refs_2_), custom_call_target="tpu_custom_call" | custom-call | tf_op jit(solution)/shard_map/scale/pallas_call | solution.py:280

commit v4 on v3

--- a/solution.py
+++ b/solution.py
@@ -10,10 +10,11 @@
 SEND = 10
 TILES = 4
 GROUP = 16
-PIECES = 8
 STEPS = 8
 SPAN = 64
-START = (((2, 0, 5),), ((2, 5, 5), (1, 0, 10), (3, 0, 10)), ())
+START = (((2, 0, 8),), (), ((2, 8, 2), (1, 0, 10), (3, 0, 10)), ())
+RING = sorted(((dz, dc) for dz in range(8) for dc in range(2) if dz or dc), key=lambda d: -2 * min(d[0], 8 - d[0]) - d[1])
+FACE = sorted(((dy, dx) for dy in range(4) for dx in range(4) if dy or dx), key=lambda d: -sum(min(v, 4 - v) for v in d))
 MESH = pl.DeviceIdType.MESH
 F32, BF16 = jnp.float32, jnp.bfloat16
 
@@ -87,59 +88,38 @@
             work[s + SPAN :, :] = work[s + SPAN :, :] - g[s + SPAN :, :]
 
 
+def total_of(terms):
+    while len(terms) > 1:
+        terms = [sum(terms[i : i + 2]) for i in range(0, len(terms), 2)]
+    return terms[0]
+
+
 def exchange(routes_hbm, x_hbm, s_hbm, placed_ref, upper_ref, inverse_ref, x_ref, s_ref, routes_ref, sk_ref, send_ref, part_ref,
-             got1_ref, got2_ref, gram_ref, work_ref, table_ref, x_sem, in_sem, put_sem, get_sem, ar_put, ar_get):
+             got1_ref, got2_ref, gram_ref, work_ref, table_ref, in_sem, put_sem, get_sem, ar_put, ar_get):
     slab, tile = lax.axis_index("slab"), lax.axis_index("tile")
     core, y, z = slab % 2, (slab // 2) % 4, slab // 8
     ring = z * 2 + core
     face = y * 4 + tile
 
-    def ring_peer(k):
-        return (((k // 2) * 4 + y) * 2 + k % 2, tile)
-
-    def face_peer(k):
-        return ((z * 4 + k // 4) * 2 + core, k % 4)
-
-    rows = x_hbm.shape[0] // PIECES
-
-    def piece(p):
-        part = pl.ds(p * rows, rows)
-        return pltpu.make_async_copy(x_hbm.at[part], x_ref.at[part], x_sem.at[p])
-
-    s_copy = pltpu.make_async_copy(s_hbm, s_ref, in_sem.at[0])
-    routes_copy = pltpu.make_async_copy(routes_hbm, routes_ref, in_sem.at[1])
+    ring_peers = []
+    for dz, dc in RING:
+        to_z, to_core = lax.rem(z + dz, 8), lax.rem(core + dc, 2)
+        ring_peers.append((to_z * 2 + to_core, ((to_z * 4 + y) * 2 + to_core, tile)))
+    face_peers = []
+    for dy, dx in FACE:
+        to_y, to_x = lax.rem(y + dy, 4), lax.rem(tile + dx, 4)
+        face_peers.append((to_y * 4 + to_x, ((z * 4 + to_y) * 2 + core, to_x)))
+
+    barrier = pltpu.get_barrier_semaphore()
+    for _, peer in ring_peers + face_peers:
+        pl.semaphore_signal(barrier, inc=1, device_id=peer, device_id_type=MESH)
+
+    x_copy = pltpu.make_async_copy(x_hbm, x_ref, in_sem.at[0])
+    s_copy = pltpu.make_async_copy(s_hbm, s_ref, in_sem.at[1])
+    routes_copy = pltpu.make_async_copy(routes_hbm, routes_ref, in_sem.at[2])
+    routes_copy.start()
     s_copy.start()
-    for p in range(PIECES):
-        piece(p).start()
-    routes_copy.start()
-
-    barrier = pltpu.get_barrier_semaphore()
-    for d in range(1, GROUP):
-        pl.semaphore_signal(barrier, inc=1, device_id=ring_peer((ring + d) % GROUP), device_id_type=MESH)
-        pl.semaphore_signal(barrier, inc=1, device_id=face_peer((face + d) % GROUP), device_id_type=MESH)
-
-    part_ref[...] = jnp.zeros_like(part_ref)
-    s_copy.wait()
-
-    @pl.loop(0, PIECES)
-    def _(p):
-        piece(p).wait()
-        wide = x_ref[pl.ds(p * rows, rows)].reshape(rows * 128, 256)
-        sk = jnp.dot(wide, s_ref[...], preferred_element_type=F32).astype(BF16)
-        sk_ref[pl.ds(p * rows, rows)] = sk.reshape(rows, 128, 128)
-        g = lax.dot_general(sk, sk, (((0,), (0,)), ((), ())), preferred_element_type=F32)
-        part_ref[...] += g.reshape(GROUP, 8, 128)
-
-    pl.semaphore_wait(barrier, 2 * (GROUP - 1))
-
-    def all_of(ref, sem):
-        return pltpu.make_async_copy(ref.at[pl.ds(0, GROUP - 1)], ref.at[pl.ds(0, GROUP - 1)], sem)
-
-    for d in range(1, GROUP):
-        to = (ring + d) % GROUP
-        pltpu.make_async_remote_copy(
-            src_ref=part_ref.at[to], dst_ref=got1_ref.at[d - 1], send_sem=ar_put.at[0], recv_sem=ar_get.at[0],
-            device_id=ring_peer(to), device_id_type=MESH).start()
+    x_copy.start()
 
     routes_copy.wait()
     masks = [jnp.int32(0)] * TILES
@@ -154,6 +134,15 @@
             table_ref[o, k] = jnp.where(m != 0, 31 - lax.clz(low), -1)
             m = m & (m - 1)
 
+    s_copy.wait()
+    x_copy.wait()
+    cells = x_ref.shape[0] * 128
+    sk = jnp.dot(x_ref[...].reshape(cells, 256), s_ref[...], preferred_element_type=F32).astype(BF16)
+    sk_ref[...] = sk.reshape(sk_ref.shape)
+
+    def all_of(ref, sem):
+        return pltpu.make_async_copy(ref.at[pl.ds(0, GROUP - 1)], ref.at[pl.ds(0, GROUP - 1)], sem)
+
     def pick(o, k):
         at = table_ref[o, k]
         block = sk_ref[jnp.maximum(at, 0)]
@@ -177,10 +166,25 @@
         def _(k):
             send_ref[d - 1, k] = pick((tile + d) % TILES, k)
 
-    for part in START[0]:
-        fill(*part)
-        transfer(*part).start()
-    for part in parts[len(START[0]):]:
+    def begin(step):
+        for part in START[step]:
+            if step < 2:
+                fill(*part)
+            transfer(*part).start()
+
+    pl.semaphore_wait(barrier, 2 * (GROUP - 1))
+    begin(0)
+    sk = sk_ref[...].reshape(cells, 128)
+    gram = lax.dot_general(sk, sk, (((0,), (0,)), ((), ())), preferred_element_type=F32)
+    part_ref[...] = gram.reshape(part_ref.shape)
+
+    for i, (to, peer) in enumerate(ring_peers):
+        pltpu.make_async_remote_copy(
+            src_ref=part_ref.at[to], dst_ref=got1_ref.at[i], send_sem=ar_put.at[0], recv_sem=ar_get.at[0],
+            device_id=peer, device_id_type=MESH).start()
+
+    begin(1)
+    for part in START[2] + START[3]:
         fill(*part)
 
     @pl.loop(0, SEND)
@@ -188,29 +192,19 @@
         placed_ref[tile, k] = pick(tile, k)
 
     all_of(got1_ref, ar_get.at[0]).wait()
-    mine = part_ref[ring]
-    for d in range(GROUP - 1):
-        mine = mine + got1_ref[d]
-    got2_ref[face] = mine
-    for d in range(1, GROUP):
-        to = (face + d) % GROUP
+    got2_ref[face] = total_of([part_ref[ring]] + [got1_ref[i] for i in range(GROUP - 1)])
+    for _, peer in face_peers:
         pltpu.make_async_remote_copy(
             src_ref=got2_ref.at[face], dst_ref=got2_ref.at[face], send_sem=ar_put.at[1], recv_sem=ar_get.at[1],
-            device_id=face_peer(to), device_id_type=MESH).start()
-    for part in START[1]:
-        transfer(*part).start()
+            device_id=peer, device_id_type=MESH).start()
+    begin(2)
     all_of(got2_ref, ar_get.at[1]).wait()
-    total = got2_ref[0]
-    for d in range(1, GROUP):
-        total = total + got2_ref[d]
-    gram_ref[ring] = total
-    for d in range(1, GROUP):
-        to = (ring + d) % GROUP
+    gram_ref[ring] = total_of([got2_ref[i] for i in range(GROUP)])
+    for _, peer in ring_peers:
         pltpu.make_async_remote_copy(
             src_ref=gram_ref.at[ring], dst_ref=gram_ref.at[ring], send_sem=ar_put.at[2], recv_sem=ar_get.at[2],
-            device_id=ring_peer(to), device_id_type=MESH).start()
-    for part in START[2]:
-        transfer(*part).start()
+            device_id=peer, device_id_type=MESH).start()
+    begin(3)
     all_of(gram_ref, ar_get.at[2]).wait()
 
     factor(gram_ref, upper_ref, inverse_ref, work_ref)
@@ -227,7 +221,7 @@
     triangle_ref[...] = jnp.where(row <= col, upper_ref[...] * (1.0 / cell_root), 0.0)
     tri = pltpu.make_async_copy(triangle_ref, triangle_hbm, tri_sem)
     tri.start()
-    h, m, l = split3(jnp.where(row >= col, inverse_ref[...] * cell_root, 0.0))
+    h, m, _ = split3(jnp.where(row >= col, inverse_ref[...] * cell_root, 0.0))
     count = placed_ref.shape[0] // STEPS
 
     def copy(i):
@@ -237,7 +231,7 @@
     for i in range(STEPS):
         part = pl.ds(i * count, count)
         rows = placed_ref[part].reshape(count * 128, 128)
-        out = sum(lax.dot_general(rows, w, (((1,), (1,)), ((), ())), preferred_element_type=F32) for w in (l, m, h))
+        out = sum(lax.dot_general(rows, w, (((1,), (1,)), ((), ())), preferred_element_type=F32) for w in (m, h))
         basis_ref[part] = out.astype(BF16).reshape(count, 128, 128)
         copy(i).start()
     tri.wait()
@@ -267,8 +261,7 @@
             pltpu.VMEM((GROUP, 8, 128), F32),
             pltpu.VMEM((128, 256), F32),
             pltpu.SMEM((TILES, SEND), jnp.int32),
-            pltpu.SemaphoreType.DMA((PIECES,)),
-            pltpu.SemaphoreType.DMA((2,)),
+            pltpu.SemaphoreType.DMA((3,)),
             pltpu.SemaphoreType.DMA((sum(map(len, START)),)),
             pltpu.SemaphoreType.DMA((sum(map(len, START)),)),
             pltpu.SemaphoreType.DMA((3,)),

time: 33.3 us -> 31.1 us (0.934)
  Pallas kernels: 32.5 us -> 30.4 us
    pallas_call x1, Pallas kernels: 30.5 us -> 28.7 us  [local(): pl.pallas_call(exchange, out_shape=(jax.ShapeDtypeStruct((TILES, SEND, 12...]
    pallas_call x1, Pallas kernels: 2 us -> 1.66 us  [local(): pl.pallas_call(lambda *refs: scale(cell_root, *refs), out_shape=(jax.Shap...]
where the time goes in v4:
time: 31.1 us; the launch traced here: 31 us
  Pallas kernels  30.4 us (98%)
  between operations  0.64 us (2%)
    pallas_call x1, Pallas kernels, local(): pl.pallas_call(exchange, out_shape=(jax.ShapeDtypeStruct((TILES, SEND, 12...  28.7 us
    pallas_call x1, Pallas kernels, local(): pl.pallas_call(lambda *refs: scale(cell_root, *refs), out_shape=(jax.Shap...  1.66 us

profile of v4, /device:TPU:1, one launch (start us, length us, event | category | flops | bytes accessed | tf_op | source)
XLA Modules:
  0.0 31.0 jit_solution(8519283994084056790)
XLA Ops:
  0.6 28.7 %exchange.1 = (bf16[4,10,128,128]{3,2,1,0:T(8,128)(2,1)S(1)}, f32[128,128]{1,0:T(8,128)S(1)}, f32[128,128]{1,0:T(8,128)S(1)}) custom-call(s32[1,32]{1,0:T(1,128)} %bitcast.3, bf16[32,128,256]{2,1,0:T(8,128)(2,1)} %x_hbm.1, bf16[256,128]{1,0:T(8,128)(2,1)} %s_hbm.1), custom_call_target="tpu_custom_call" | custom-call | tf_op jit(solution)/shard_map/exchange/pallas_call | solution.py:247
  29.3 1.7 %scale.1 = (bf16[40,128,128]{2,1,0:T(8,128)(2,1)}, f32[128,128]{1,0:T(8,128)}) custom-call(bf16[40,128,128]{2,1,0:T(8,128)(2,1)S(1)} %bitcast.2, f32[128,128]{1,0:T(8,128)S(1)} %get-tuple-element.6.refs_1_, f32[128,128]{1,0:T(8,128)S(1)} %get-tuple-element.7.refs_2_), custom_call_target="tpu_custom_call" | custom-call | tf_op jit(solution)/shard_map/scale/pallas_call | solution.py:273

commit v5 on v4

--- a/solution.py
+++ b/solution.py
@@ -12,7 +12,7 @@
 GROUP = 16
 STEPS = 8
 SPAN = 64
-START = (((2, 0, 8),), (), ((2, 8, 2), (1, 0, 10), (3, 0, 10)), ())
+START = (((2, 0, 6),), ((1, 0, 10), (3, 0, 10)), ((2, 6, 4),))
 RING = sorted(((dz, dc) for dz in range(8) for dc in range(2) if dz or dc), key=lambda d: -2 * min(d[0], 8 - d[0]) - d[1])
 FACE = sorted(((dy, dx) for dy in range(4) for dx in range(4) if dy or dx), key=lambda d: -sum(min(v, 4 - v) for v in d))
 MESH = pl.DeviceIdType.MESH
@@ -96,6 +96,13 @@
 
 def exchange(routes_hbm, x_hbm, s_hbm, placed_ref, upper_ref, inverse_ref, x_ref, s_ref, routes_ref, sk_ref, send_ref, part_ref,
              got1_ref, got2_ref, gram_ref, work_ref, table_ref, in_sem, put_sem, get_sem, ar_put, ar_get):
+    x_copy = pltpu.make_async_copy(x_hbm, x_ref, in_sem.at[0])
+    s_copy = pltpu.make_async_copy(s_hbm, s_ref, in_sem.at[1])
+    routes_copy = pltpu.make_async_copy(routes_hbm, routes_ref, in_sem.at[2])
+    routes_copy.start()
+    s_copy.start()
+    x_copy.start()
+
     slab, tile = lax.axis_index("slab"), lax.axis_index("tile")
     core, y, z = slab % 2, (slab // 2) % 4, slab // 8
     ring = z * 2 + core
@@ -113,13 +120,6 @@
     barrier = pltpu.get_barrier_semaphore()
     for _, peer in ring_peers + face_peers:
         pl.semaphore_signal(barrier, inc=1, device_id=peer, device_id_type=MESH)
-
-    x_copy = pltpu.make_async_copy(x_hbm, x_ref, in_sem.at[0])
-    s_copy = pltpu.make_async_copy(s_hbm, s_ref, in_sem.at[1])
-    routes_copy = pltpu.make_async_copy(routes_hbm, routes_ref, in_sem.at[2])
-    routes_copy.start()
-    s_copy.start()
-    x_copy.start()
 
     routes_copy.wait()
     masks = [jnp.int32(0)] * TILES
@@ -168,23 +168,21 @@
 
     def begin(step):
         for part in START[step]:
-            if step < 2:
+            if step == 0:
                 fill(*part)
             transfer(*part).start()
 
-    pl.semaphore_wait(barrier, 2 * (GROUP - 1))
-    begin(0)
-    sk = sk_ref[...].reshape(cells, 128)
     gram = lax.dot_general(sk, sk, (((0,), (0,)), ((), ())), preferred_element_type=F32)
     part_ref[...] = gram.reshape(part_ref.shape)
+    pl.semaphore_wait(barrier, 2 * (GROUP - 1))
 
     for i, (to, peer) in enumerate(ring_peers):
         pltpu.make_async_remote_copy(
             src_ref=part_ref.at[to], dst_ref=got1_ref.at[i], send_sem=ar_put.at[0], recv_sem=ar_get.at[0],
             device_id=peer, device_id_type=MESH).start()
 
-    begin(1)
-    for part in START[2] + START[3]:
+    begin(0)
+    for part in START[1] + START[2]:
         fill(*part)
 
     @pl.loop(0, SEND)
@@ -197,14 +195,14 @@
         pltpu.make_async_remote_copy(
             src_ref=got2_ref.at[face], dst_ref=got2_ref.at[face], send_sem=ar_put.at[1], recv_sem=ar_get.at[1],
             device_id=peer, device_id_type=MESH).start()
-    begin(2)
+    begin(1)
     all_of(got2_ref, ar_get.at[1]).wait()
     gram_ref[ring] = total_of([got2_ref[i] for i in range(GROUP)])
     for _, peer in ring_peers:
         pltpu.make_async_remote_copy(
             src_ref=gram_ref.at[ring], dst_ref=gram_ref.at[ring], send_sem=ar_put.at[2], recv_sem=ar_get.at[2],
             device_id=peer, device_id_type=MESH).start()
-    begin(3)
+    begin(2)
     all_of(gram_ref, ar_get.at[2]).wait()
 
     factor(gram_ref, upper_ref, inverse_ref, work_ref)

time: 31.1 us -> 30.1 us (0.968)
  Pallas kernels: 30.4 us -> 29.3 us
    pallas_call x1, Pallas kernels: 28.7 us -> 27.7 us  [local(): pl.pallas_call(exchange, out_shape=(jax.ShapeDtypeStruct((TILES, SEND, 12...]
where the time goes in v5:
time: 30.1 us; the launch traced here: 30 us
  Pallas kernels  29.3 us (97%)
  between operations  0.64 us (2%)
    pallas_call x1, Pallas kernels, local(): pl.pallas_call(exchange, out_shape=(jax.ShapeDtypeStruct((TILES, SEND, 12...  27.7 us
    pallas_call x1, Pallas kernels, local(): pl.pallas_call(lambda *refs: scale(cell_root, *refs), out_shape=(jax.Shap...  1.66 us

profile of v5, /device:TPU:1, one launch (start us, length us, event | category | flops | bytes accessed | tf_op | source)
XLA Modules:
  0.0 30.0 jit_solution(9430700278505896837)
XLA Ops:
  0.6 27.7 %exchange.1 = (bf16[4,10,128,128]{3,2,1,0:T(8,128)(2,1)S(1)}, f32[128,128]{1,0:T(8,128)S(1)}, f32[128,128]{1,0:T(8,128)S(1)}) custom-call(s32[1,32]{1,0:T(1,128)} %bitcast.3, bf16[32,128,256]{2,1,0:T(8,128)(2,1)} %x_hbm.1, bf16[256,128]{1,0:T(8,128)(2,1)} %s_hbm.1), custom_call_target="tpu_custom_call" | custom-call | tf_op jit(solution)/shard_map/exchange/pallas_call | solution.py:245
  28.3 1.7 %scale.1 = (bf16[40,128,128]{2,1,0:T(8,128)(2,1)}, f32[128,128]{1,0:T(8,128)}) custom-call(bf16[40,128,128]{2,1,0:T(8,128)(2,1)S(1)} %bitcast.2, f32[128,128]{1,0:T(8,128)S(1)} %get-tuple-element.6.refs_1_, f32[128,128]{1,0:T(8,128)S(1)} %get-tuple-element.7.refs_2_), custom_call_target="tpu_custom_call" | custom-call | tf_op jit(solution)/shard_map/scale/pallas_call | solution.py:271

commit v6 on v5

--- a/solution.py
+++ b/solution.py
@@ -12,7 +12,7 @@
 GROUP = 16
 STEPS = 8
 SPAN = 64
-START = (((2, 0, 6),), ((1, 0, 10), (3, 0, 10)), ((2, 6, 4),))
+START = (((2, 0, 7),), ((1, 0, 10), (3, 0, 10)), ((2, 7, 3),))
 RING = sorted(((dz, dc) for dz in range(8) for dc in range(2) if dz or dc), key=lambda d: -2 * min(d[0], 8 - d[0]) - d[1])
 FACE = sorted(((dy, dx) for dy in range(4) for dx in range(4) if dy or dx), key=lambda d: -sum(min(v, 4 - v) for v in d))
 MESH = pl.DeviceIdType.MESH
@@ -45,14 +45,16 @@
     return jnp.concatenate([v, v], 1)
 
 
-def factor(gram_ref, upper_ref, inverse_ref, work):
-    row = lax.broadcasted_iota(jnp.int32, (128, 128), 0)
-    col = lax.broadcasted_iota(jnp.int32, (128, 128), 1)
-    work[:, :128] = gram_ref[...].reshape(128, 128)
-    work[:, 128:] = (row == col).astype(F32)
+def factor(gram_ref, upper_ref, inverse_ref, arrive):
+    row = lax.broadcasted_iota(jnp.int32, (8, 128), 0)
+    col = lax.broadcasted_iota(jnp.int32, (8, 128), 1)
     sub = lax.broadcasted_iota(jnp.int32, (8, 256), 0)
+    product = None
     for s in range(0, 128, SPAN):
-        rows = {q: work[q : q + 8, :] for q in range(s, s + SPAN, 8)}
+        arrive(s // SPAN)
+        rows = {q: jnp.concatenate([gram_ref[q // 8], (row + q == col).astype(F32)], 1) for q in range(s, s + SPAN, 8)}
+        if s:
+            rows = {q: v - product[q : q + 8] for q, v in rows.items()}
         own = columns(rows[s], s)
         done = []
         for p in range(s, s + SPAN, 8):
@@ -84,8 +86,7 @@
             inverse_ref[p : p + 8, :] = u[:, 128:]
             done.append(u)
         if s + SPAN < 128:
-            g = outer_products(jnp.concatenate(done, 0))
-            work[s + SPAN :, :] = work[s + SPAN :, :] - g[s + SPAN :, :]
+            product = outer_products(jnp.concatenate(done, 0))
 
 
 def total_of(terms):
@@ -95,31 +96,75 @@
 
 
 def exchange(routes_hbm, x_hbm, s_hbm, placed_ref, upper_ref, inverse_ref, x_ref, s_ref, routes_ref, sk_ref, send_ref, part_ref,
-             got1_ref, got2_ref, gram_ref, work_ref, table_ref, in_sem, put_sem, get_sem, ar_put, ar_get):
+             got1_ref, got2_ref, gram_ref, sum_ref, table_ref, in_sem, put_sem, get_sem, ar_put, ar_get, half_get):
+    slab, tile = lax.axis_index("slab"), lax.axis_index("tile")
+    core, y, z = slab % 2, (slab // 2) % 4, slab // 8
+    ring = z * 2 + core
+    face = y * 4 + tile
+
+    barrier = pltpu.get_barrier_semaphore()
+    ring_peers, face_peers = [], []
+    for dz, dc in RING:
+        to_z, to_core = lax.rem(z + dz, 8), lax.rem(core + dc, 2)
+        ring_peers.append((to_z * 2 + to_core, ((to_z * 4 + y) * 2 + to_core, tile)))
+        pl.semaphore_signal(barrier, inc=1, device_id=ring_peers[-1][1], device_id_type=MESH)
     x_copy = pltpu.make_async_copy(x_hbm, x_ref, in_sem.at[0])
     s_copy = pltpu.make_async_copy(s_hbm, s_ref, in_sem.at[1])
     routes_copy = pltpu.make_async_copy(routes_hbm, routes_ref, in_sem.at[2])
     routes_copy.start()
     s_copy.start()
     x_copy.start()
-
-    slab, tile = lax.axis_index("slab"), lax.axis_index("tile")
-    core, y, z = slab % 2, (slab // 2) % 4, slab // 8
-    ring = z * 2 + core
-    face = y * 4 + tile
-
-    ring_peers = []
-    for dz, dc in RING:
-        to_z, to_core = lax.rem(z + dz, 8), lax.rem(core + dc, 2)
-        ring_peers.append((to_z * 2 + to_core, ((to_z * 4 + y) * 2 + to_core, tile)))
-    face_peers = []
     for dy, dx in FACE:
         to_y, to_x = lax.rem(y + dy, 4), lax.rem(tile + dx, 4)
         face_peers.append((to_y * 4 + to_x, ((z * 4 + to_y) * 2 + core, to_x)))
-
-    barrier = pltpu.get_barrier_semaphore()
-    for _, peer in ring_peers + face_peers:
-        pl.semaphore_signal(barrier, inc=1, device_id=peer, device_id_type=MESH)
+        pl.semaphore_signal(barrier, inc=1, device_id=face_peers[-1][1], device_id_type=MESH)
+
+    s_copy.wait()
+    x_copy.wait()
+    cells = x_ref.shape[0] * 128
+    sk = jnp.dot(x_ref[...].reshape(cells, 256), s_ref[...], preferred_element_type=F32).astype(BF16)
+    sk_ref[...] = sk.reshape(sk_ref.shape)
+
+    def all_of(ref, sem):
+        return pltpu.make_async_copy(ref.at[pl.ds(0, GROUP - 1)], ref.at[pl.ds(0, GROUP - 1)], sem)
+
+    def pick(o, k):
+        at = table_ref[o, k]
+        block = sk_ref[jnp.maximum(at, 0)]
+        return jnp.where(at >= 0, block, jnp.zeros_like(block))
+
+    parts = [part for step in START for part in step]
+
+    def transfer(d, first, count):
+        at = parts.index((d, first, count))
+        return pltpu.make_async_remote_copy(
+            src_ref=send_ref.at[d - 1, pl.ds(first, count)],
+            dst_ref=placed_ref.at[tile, pl.ds(first, count)],
+            send_sem=put_sem.at[at],
+            recv_sem=get_sem.at[at],
+            device_id=(slab, (tile + d) % TILES),
+            device_id_type=MESH,
+        )
+
+    def fill(d, first, count):
+        @pl.loop(first, first + count)
+        def _(k):
+            send_ref[d - 1, k] = pick((tile + d) % TILES, k)
+
+    def begin(step):
+        for part in START[step]:
+            if step == 0:
+                fill(*part)
+            transfer(*part).start()
+
+    gram = lax.dot_general(sk, sk, (((0,), (0,)), ((), ())), preferred_element_type=F32)
+    part_ref[...] = gram.reshape(part_ref.shape)
+    pl.semaphore_wait(barrier, 2 * (GROUP - 1))
+
+    for i, (to, peer) in enumerate(ring_peers):
+        pltpu.make_async_remote_copy(
+            src_ref=part_ref.at[to], dst_ref=got1_ref.at[i], send_sem=ar_put.at[0], recv_sem=ar_get.at[0],
+            device_id=peer, device_id_type=MESH).start()
 
     routes_copy.wait()
     masks = [jnp.int32(0)] * TILES
@@ -134,53 +179,6 @@
             table_ref[o, k] = jnp.where(m != 0, 31 - lax.clz(low), -1)
             m = m & (m - 1)
 
-    s_copy.wait()
-    x_copy.wait()
-    cells = x_ref.shape[0] * 128
-    sk = jnp.dot(x_ref[...].reshape(cells, 256), s_ref[...], preferred_element_type=F32).astype(BF16)
-    sk_ref[...] = sk.reshape(sk_ref.shape)
-
-    def all_of(ref, sem):
-        return pltpu.make_async_copy(ref.at[pl.ds(0, GROUP - 1)], ref.at[pl.ds(0, GROUP - 1)], sem)
-
-    def pick(o, k):
-        at = table_ref[o, k]
-        block = sk_ref[jnp.maximum(at, 0)]
-        return jnp.where(at >= 0, block, jnp.zeros_like(block))
-
-    parts = [part for step in START for part in step]
-
-    def transfer(d, first, count):
-        at = parts.index((d, first, count))
-        return pltpu.make_async_remote_copy(
-            src_ref=send_ref.at[d - 1, pl.ds(first, count)],
-            dst_ref=placed_ref.at[tile, pl.ds(first, count)],
-            send_sem=put_sem.at[at],
-            recv_sem=get_sem.at[at],
-            device_id=(slab, (tile + d) % TILES),
-            device_id_type=MESH,
-        )
-
-    def fill(d, first, count):
-        @pl.loop(first, first + count)
-        def _(k):
-            send_ref[d - 1, k] = pick((tile + d) % TILES, k)
-
-    def begin(step):
-        for part in START[step]:
-            if step == 0:
-                fill(*part)
-            transfer(*part).start()
-
-    gram = lax.dot_general(sk, sk, (((0,), (0,)), ((), ())), preferred_element_type=F32)
-    part_ref[...] = gram.reshape(part_ref.shape)
-    pl.semaphore_wait(barrier, 2 * (GROUP - 1))
-
-    for i, (to, peer) in enumerate(ring_peers):
-        pltpu.make_async_remote_copy(
-            src_ref=part_ref.at[to], dst_ref=got1_ref.at[i], send_sem=ar_put.at[0], recv_sem=ar_get.at[0],
-            device_id=peer, device_id_type=MESH).start()
-
     begin(0)
     for part in START[1] + START[2]:
         fill(*part)
@@ -197,15 +195,20 @@
             device_id=peer, device_id_type=MESH).start()
     begin(1)
     all_of(got2_ref, ar_get.at[1]).wait()
-    gram_ref[ring] = total_of([got2_ref[i] for i in range(GROUP)])
+    sum_ref[...] = total_of([got2_ref[i] for i in range(GROUP)])
+    half = ring // (GROUP // 2)
     for _, peer in ring_peers:
         pltpu.make_async_remote_copy(
-            src_ref=gram_ref.at[ring], dst_ref=gram_ref.at[ring], send_sem=ar_put.at[2], recv_sem=ar_get.at[2],
+            src_ref=sum_ref, dst_ref=gram_ref.at[ring], send_sem=ar_put.at[2], recv_sem=half_get.at[half],
             device_id=peer, device_id_type=MESH).start()
+    pltpu.make_async_copy(sum_ref, gram_ref.at[ring], half_get.at[half]).start()
     begin(2)
-    all_of(gram_ref, ar_get.at[2]).wait()
-
-    factor(gram_ref, upper_ref, inverse_ref, work_ref)
+
+    def arrive(i):
+        part = gram_ref.at[pl.ds(i * (GROUP // 2), GROUP // 2)]
+        pltpu.make_async_copy(part, part, half_get.at[i]).wait()
+
+    factor(gram_ref, upper_ref, inverse_ref, arrive)
 
     for i in range(3):
         all_of(got1_ref, ar_put.at[i]).wait()
@@ -257,13 +260,14 @@
             pltpu.VMEM((GROUP, 8, 128), F32),
             pltpu.VMEM((GROUP, 8, 128), F32),
             pltpu.VMEM((GROUP, 8, 128), F32),
-            pltpu.VMEM((128, 256), F32),
+            pltpu.VMEM((8, 128), F32),
             pltpu.SMEM((TILES, SEND), jnp.int32),
             pltpu.SemaphoreType.DMA((3,)),
             pltpu.SemaphoreType.DMA((sum(map(len, START)),)),
             pltpu.SemaphoreType.DMA((sum(map(len, START)),)),
             pltpu.SemaphoreType.DMA((3,)),
-            pltpu.SemaphoreType.DMA((3,)),
+            pltpu.SemaphoreType.DMA((2,)),
+            pltpu.SemaphoreType.DMA((2,)),
         ],
         compiler_params=pltpu.CompilerParams(collective_id=0, has_side_effects=True, vmem_limit_bytes=32 * 2**20),
         name="exchange",

time: 30.1 us -> 29.4 us (0.977)
  Pallas kernels: 29.3 us -> 28.7 us
    pallas_call x1, Pallas kernels: 27.7 us -> 27 us  [local(): pl.pallas_call(exchange, out_shape=(jax.ShapeDtypeStruct((TILES, SEND, 12...]
where the time goes in v6:
time: 29.4 us; the launch traced here: 29.3 us
  Pallas kernels  28.7 us (98%)
  between operations  0.64 us (2%)
    pallas_call x1, Pallas kernels, local(): pl.pallas_call(exchange, out_shape=(jax.ShapeDtypeStruct((TILES, SEND, 12...  27 us
    pallas_call x1, Pallas kernels, local(): pl.pallas_call(lambda *refs: scale(cell_root, *refs), out_shape=(jax.Shap...  1.66 us

profile of v6, /device:TPU:1, one launch (start us, length us, event | category | flops | bytes accessed | tf_op | source)
XLA Modules:
  0.0 29.3 jit_solution(13486074470159052810)
XLA Ops:
  0.6 27.0 %exchange.1 = (bf16[4,10,128,128]{3,2,1,0:T(8,128)(2,1)S(1)}, f32[128,128]{1,0:T(8,128)S(1)}, f32[128,128]{1,0:T(8,128)S(1)}) custom-call(s32[1,32]{1,0:T(1,128)} %bitcast.3, bf16[32,128,256]{2,1,0:T(8,128)(2,1)} %x_hbm.1, bf16[256,128]{1,0:T(8,128)(2,1)} %s_hbm.1), custom_call_target="tpu_custom_call" | custom-call | tf_op jit(solution)/shard_map/exchange/pallas_call | solution.py:248
  27.6 1.7 %scale.1 = (bf16[40,128,128]{2,1,0:T(8,128)(2,1)}, f32[128,128]{1,0:T(8,128)}) custom-call(bf16[40,128,128]{2,1,0:T(8,128)(2,1)S(1)} %bitcast.2, f32[128,128]{1,0:T(8,128)S(1)} %get-tuple-element.6.refs_1_, f32[128,128]{1,0:T(8,128)S(1)} %get-tuple-element.7.refs_2_), custom_call_target="tpu_custom_call" | custom-call | tf_op jit(solution)/shard_map/scale/pallas_call | solution.py:275

commit v7 on v6

--- a/solution.py
+++ b/solution.py
@@ -119,53 +119,6 @@
         face_peers.append((to_y * 4 + to_x, ((z * 4 + to_y) * 2 + core, to_x)))
         pl.semaphore_signal(barrier, inc=1, device_id=face_peers[-1][1], device_id_type=MESH)
 
-    s_copy.wait()
-    x_copy.wait()
-    cells = x_ref.shape[0] * 128
-    sk = jnp.dot(x_ref[...].reshape(cells, 256), s_ref[...], preferred_element_type=F32).astype(BF16)
-    sk_ref[...] = sk.reshape(sk_ref.shape)
-
-    def all_of(ref, sem):
-        return pltpu.make_async_copy(ref.at[pl.ds(0, GROUP - 1)], ref.at[pl.ds(0, GROUP - 1)], sem)
-
-    def pick(o, k):
-        at = table_ref[o, k]
-        block = sk_ref[jnp.maximum(at, 0)]
-        return jnp.where(at >= 0, block, jnp.zeros_like(block))
-
-    parts = [part for step in START for part in step]
-
-    def transfer(d, first, count):
-        at = parts.index((d, first, count))
-        return pltpu.make_async_remote_copy(
-            src_ref=send_ref.at[d - 1, pl.ds(first, count)],
-            dst_ref=placed_ref.at[tile, pl.ds(first, count)],
-            send_sem=put_sem.at[at],
-            recv_sem=get_sem.at[at],
-            device_id=(slab, (tile + d) % TILES),
-            device_id_type=MESH,
-        )
-
-    def fill(d, first, count):
-        @pl.loop(first, first + count)
-        def _(k):
-            send_ref[d - 1, k] = pick((tile + d) % TILES, k)
-
-    def begin(step):
-        for part in START[step]:
-            if step == 0:
-                fill(*part)
-            transfer(*part).start()
-
-    gram = lax.dot_general(sk, sk, (((0,), (0,)), ((), ())), preferred_element_type=F32)
-    part_ref[...] = gram.reshape(part_ref.shape)
-    pl.semaphore_wait(barrier, 2 * (GROUP - 1))
-
-    for i, (to, peer) in enumerate(ring_peers):
-        pltpu.make_async_remote_copy(
-            src_ref=part_ref.at[to], dst_ref=got1_ref.at[i], send_sem=ar_put.at[0], recv_sem=ar_get.at[0],
-            device_id=peer, device_id_type=MESH).start()
-
     routes_copy.wait()
     masks = [jnp.int32(0)] * TILES
     for j in range(32):
@@ -179,7 +132,54 @@
             table_ref[o, k] = jnp.where(m != 0, 31 - lax.clz(low), -1)
             m = m & (m - 1)
 
+    s_copy.wait()
+    x_copy.wait()
+    cells = x_ref.shape[0] * 128
+    sk = jnp.dot(x_ref[...].reshape(cells, 256), s_ref[...], preferred_element_type=F32).astype(BF16)
+    sk_ref[...] = sk.reshape(sk_ref.shape)
+
+    def all_of(ref, sem):
+        return pltpu.make_async_copy(ref.at[pl.ds(0, GROUP - 1)], ref.at[pl.ds(0, GROUP - 1)], sem)
+
+    def pick(o, k):
+        at = table_ref[o, k]
+        block = sk_ref[jnp.maximum(at, 0)]
+        return jnp.where(at >= 0, block, jnp.zeros_like(block))
+
+    parts = [part for step in START for part in step]
+
+    def transfer(d, first, count):
+        at = parts.index((d, first, count))
+        return pltpu.make_async_remote_copy(
+            src_ref=send_ref.at[d - 1, pl.ds(first, count)],
+            dst_ref=placed_ref.at[tile, pl.ds(first, count)],
+            send_sem=put_sem.at[at],
+            recv_sem=get_sem.at[at],
+            device_id=(slab, (tile + d) % TILES),
+            device_id_type=MESH,
+        )
+
+    def fill(d, first, count):
+        @pl.loop(first, first + count)
+        def _(k):
+            send_ref[d - 1, k] = pick((tile + d) % TILES, k)
+
+    def begin(step):
+        for part in START[step]:
+            transfer(*part).start()
+
+    gram = lax.dot_general(sk, sk, (((0,), (0,)), ((), ())), preferred_element_type=F32)
+    part_ref[...] = gram.reshape(part_ref.shape)
+    for part in START[0]:
+        fill(*part)
+    pl.semaphore_wait(barrier, 2 * (GROUP - 1))
+
     begin(0)
+    for i, (to, peer) in enumerate(ring_peers):
+        pltpu.make_async_remote_copy(
+            src_ref=part_ref.at[to], dst_ref=got1_ref.at[i], send_sem=ar_put.at[0], recv_sem=ar_get.at[0],
+            device_id=peer, device_id_type=MESH).start()
+
     for part in START[1] + START[2]:
         fill(*part)
 

time: 29.4 us -> 29.3 us (level)
  no operation moved by 1% of the time
where the time goes in v7:
time: 29.3 us; the launch traced here: 29.2 us
  Pallas kernels  28.6 us (98%)
  between operations  0.64 us (2%)
    pallas_call x1, Pallas kernels, local(): pl.pallas_call(exchange, out_shape=(jax.ShapeDtypeStruct((TILES, SEND, 12...  26.9 us
    pallas_call x1, Pallas kernels, local(): pl.pallas_call(lambda *refs: scale(cell_root, *refs), out_shape=(jax.Shap...  1.66 us

profile of v7, /device:TPU:1, one launch (start us, length us, event | category | flops | bytes accessed | tf_op | source)
XLA Modules:
  0.0 29.2 jit_solution(16315349712152622763)
XLA Ops:
  0.6 26.9 %exchange.1 = (bf16[4,10,128,128]{3,2,1,0:T(8,128)(2,1)S(1)}, f32[128,128]{1,0:T(8,128)S(1)}, f32[128,128]{1,0:T(8,128)S(1)}) custom-call(s32[1,32]{1,0:T(1,128)} %bitcast.3, bf16[32,128,256]{2,1,0:T(8,128)(2,1)} %x_hbm.1, bf16[256,128]{1,0:T(8,128)(2,1)} %s_hbm.1), custom_call_target="tpu_custom_call" | custom-call | tf_op jit(solution)/shard_map/exchange/pallas_call | solution.py:248
  27.6 1.7 %scale.1 = (bf16[40,128,128]{2,1,0:T(8,128)(2,1)}, f32[128,128]{1,0:T(8,128)}) custom-call(bf16[40,128,128]{2,1,0:T(8,128)(2,1)S(1)} %bitcast.2, f32[128,128]{1,0:T(8,128)S(1)} %get-tuple-element.6.refs_1_, f32[128,128]{1,0:T(8,128)S(1)} %get-tuple-element.7.refs_2_), custom_call_target="tpu_custom_call" | custom-call | tf_op jit(solution)/shard_map/scale/pallas_call | solution.py:275

commit v8 on v7

--- a/solution.py
+++ b/solution.py
@@ -11,7 +11,8 @@
 TILES = 4
 GROUP = 16
 STEPS = 8
-SPAN = 64
+SPAN = 32
+PANELS = SPAN // 8
 START = (((2, 0, 7),), ((1, 0, 10), (3, 0, 10)), ((2, 7, 3),))
 RING = sorted(((dz, dc) for dz in range(8) for dc in range(2) if dz or dc), key=lambda d: -2 * min(d[0], 8 - d[0]) - d[1])
 FACE = sorted(((dy, dx) for dy in range(4) for dx in range(4) if dy or dx), key=lambda d: -sum(min(v, 4 - v) for v in d))
@@ -86,7 +87,8 @@
             inverse_ref[p : p + 8, :] = u[:, 128:]
             done.append(u)
         if s + SPAN < 128:
-            product = outer_products(jnp.concatenate(done, 0))
+            new = outer_products(jnp.concatenate(done, 0))
+            product = new if product is None else product + new
 
 
 def total_of(terms):
@@ -96,7 +98,7 @@
 
 
 def exchange(routes_hbm, x_hbm, s_hbm, placed_ref, upper_ref, inverse_ref, x_ref, s_ref, routes_ref, sk_ref, send_ref, part_ref,
-             got1_ref, got2_ref, gram_ref, sum_ref, table_ref, in_sem, put_sem, get_sem, ar_put, ar_get, half_get):
+             got1_ref, got2_ref, gram_ref, sum_ref, table_ref, in_sem, put_sem, get_sem, ar_put, ar_get, share_get):
     slab, tile = lax.axis_index("slab"), lax.axis_index("tile")
     core, y, z = slab % 2, (slab // 2) % 4, slab // 8
     ring = z * 2 + core
@@ -196,17 +198,17 @@
     begin(1)
     all_of(got2_ref, ar_get.at[1]).wait()
     sum_ref[...] = total_of([got2_ref[i] for i in range(GROUP)])
-    half = ring // (GROUP // 2)
+    share = ring // PANELS
     for _, peer in ring_peers:
         pltpu.make_async_remote_copy(
-            src_ref=sum_ref, dst_ref=gram_ref.at[ring], send_sem=ar_put.at[2], recv_sem=half_get.at[half],
+            src_ref=sum_ref, dst_ref=gram_ref.at[ring], send_sem=ar_put.at[2], recv_sem=share_get.at[share],
             device_id=peer, device_id_type=MESH).start()
-    pltpu.make_async_copy(sum_ref, gram_ref.at[ring], half_get.at[half]).start()
+    pltpu.make_async_copy(sum_ref, gram_ref.at[ring], share_get.at[share]).start()
     begin(2)
 
     def arrive(i):
-        part = gram_ref.at[pl.ds(i * (GROUP // 2), GROUP // 2)]
-        pltpu.make_async_copy(part, part, half_get.at[i]).wait()
+        part = gram_ref.at[pl.ds(i * PANELS, PANELS)]
+        pltpu.make_async_copy(part, part, share_get.at[i]).wait()
 
     factor(gram_ref, upper_ref, inverse_ref, arrive)
 
@@ -267,7 +269,7 @@
             pltpu.SemaphoreType.DMA((sum(map(len, START)),)),
             pltpu.SemaphoreType.DMA((3,)),
             pltpu.SemaphoreType.DMA((2,)),
-            pltpu.SemaphoreType.DMA((2,)),
+            pltpu.SemaphoreType.DMA((GROUP // PANELS,)),
         ],
         compiler_params=pltpu.CompilerParams(collective_id=0, has_side_effects=True, vmem_limit_bytes=32 * 2**20),
         name="exchange",

time: 29.3 us -> 29.3 us (level)
  no operation moved by 1% of the time
where the time goes in v8:
time: 29.3 us; the launch traced here: 29.2 us
  Pallas kernels  28.6 us (98%)
  between operations  0.64 us (2%)
    pallas_call x1, Pallas kernels, local(): pl.pallas_call(exchange, out_shape=(jax.ShapeDtypeStruct((TILES, SEND, 12...  26.9 us
    pallas_call x1, Pallas kernels, local(): pl.pallas_call(lambda *refs: scale(cell_root, *refs), out_shape=(jax.Shap...  1.66 us

profile of v8, /device:TPU:1, one launch (start us, length us, event | category | flops | bytes accessed | tf_op | source)
XLA Modules:
  0.0 29.2 jit_solution(7456025397820495977)
XLA Ops:
  0.6 26.9 %exchange.1 = (bf16[4,10,128,128]{3,2,1,0:T(8,128)(2,1)S(1)}, f32[128,128]{1,0:T(8,128)S(1)}, f32[128,128]{1,0:T(8,128)S(1)}) custom-call(s32[1,32]{1,0:T(1,128)} %bitcast.3, bf16[32,128,256]{2,1,0:T(8,128)(2,1)} %x_hbm.1, bf16[256,128]{1,0:T(8,128)(2,1)} %s_hbm.1), custom_call_target="tpu_custom_call" | custom-call | tf_op jit(solution)/shard_map/exchange/pallas_call | solution.py:250
  27.6 1.7 %scale.1 = (bf16[40,128,128]{2,1,0:T(8,128)(2,1)}, f32[128,128]{1,0:T(8,128)}) custom-call(bf16[40,128,128]{2,1,0:T(8,128)(2,1)S(1)} %bitcast.2, f32[128,128]{1,0:T(8,128)S(1)} %get-tuple-element.6.refs_1_, f32[128,128]{1,0:T(8,128)S(1)} %get-tuple-element.7.refs_2_), custom_call_target="tpu_custom_call" | custom-call | tf_op jit(solution)/shard_map/scale/pallas_call | solution.py:277

commit v9 on v8

--- a/solution.py
+++ b/solution.py
@@ -161,8 +161,8 @@
             device_id_type=MESH,
         )
 
-    def fill(d, first, count):
-        @pl.loop(first, first + count)
+    def fill(d, first, count, unroll=1):
+        @pl.loop(first, first + count, unroll=unroll)
         def _(k):
             send_ref[d - 1, k] = pick((tile + d) % TILES, k)
 
@@ -173,7 +173,7 @@
     gram = lax.dot_general(sk, sk, (((0,), (0,)), ((), ())), preferred_element_type=F32)
     part_ref[...] = gram.reshape(part_ref.shape)
     for part in START[0]:
-        fill(*part)
+        fill(*part, unroll=part[2])
     pl.semaphore_wait(barrier, 2 * (GROUP - 1))
 
     begin(0)

time: 29.3 us -> 29.3 us (level)
  no operation moved by 1% of the time
where the time goes in v9:
time: 29.3 us; the launch traced here: 29.2 us
  Pallas kernels  28.6 us (98%)
  between operations  0.64 us (2%)
    pallas_call x1, Pallas kernels, local(): pl.pallas_call(exchange, out_shape=(jax.ShapeDtypeStruct((TILES, SEND, 12...  26.9 us
    pallas_call x1, Pallas kernels, local(): pl.pallas_call(lambda *refs: scale(cell_root, *refs), out_shape=(jax.Shap...  1.66 us

profile of v9, /device:TPU:1, one launch (start us, length us, event | category | flops | bytes accessed | tf_op | source)
XLA Modules:
  0.0 29.2 jit_solution(10052613887209117367)
XLA Ops:
  0.6 26.9 %exchange.1 = (bf16[4,10,128,128]{3,2,1,0:T(8,128)(2,1)S(1)}, f32[128,128]{1,0:T(8,128)S(1)}, f32[128,128]{1,0:T(8,128)S(1)}) custom-call(s32[1,32]{1,0:T(1,128)} %bitcast.3, bf16[32,128,256]{2,1,0:T(8,128)(2,1)} %x_hbm.1, bf16[256,128]{1,0:T(8,128)(2,1)} %s_hbm.1), custom_call_target="tpu_custom_call" | custom-call | tf_op jit(solution)/shard_map/exchange/pallas_call | solution.py:250
  27.6 1.7 %scale.1 = (bf16[40,128,128]{2,1,0:T(8,128)(2,1)}, f32[128,128]{1,0:T(8,128)}) custom-call(bf16[40,128,128]{2,1,0:T(8,128)(2,1)S(1)} %bitcast.2, f32[128,128]{1,0:T(8,128)S(1)} %get-tuple-element.6.refs_1_, f32[128,128]{1,0:T(8,128)S(1)} %get-tuple-element.7.refs_2_), custom_call_target="tpu_custom_call" | custom-call | tf_op jit(solution)/shard_map/scale/pallas_call | solution.py:277
